TPU v7x, 32 devices: a whole 2x2x4 slice. The times are simulated.
32 devices in a mesh: groups: 2 (over y), traj: 16 (over z, x, core).
Axes of the slice: x: 2, y: 2, z: 4, core: 2. Of those that a mesh axis runs over, the one named last changes fastest.
Arguments:
- trajectories: bfloat16 [16384, 192], P(('groups', 'traj')), parts along dimension 0
- landmark_index: int32 [1024], P(('groups', 'traj')), parts along dimension 0, may hold values from 0 to 8191, as said below
- start_vectors: float32 [16384, 32], P(('groups', 'traj')), parts along dimension 0, may hold values from -6 to 6
Outputs:
- embedding: float32 [16384, 32], P(('groups', 'traj')), parts along dimension 0
There are 2 independent parts, one for each index of `groups`. A program takes and returns all parts, laid end to end along the dimension named above; each array names one. Nothing has to cross between parts.
Inputs may be any that keep to these rules, and one draw needn't show every extreme that they name: `landmark_index`: entries b * 32 to (b + 1) * 32 - 1 are distinct rows of the range b * 512 to (b + 1) * 512 - 1, for every b.
All inputs are finite; a program needn't handle non-finite values.
Results may differ from a plain program's by a relative error of at most 0.0003.
Values may be sent and summed in bfloat16 or wider, within the bound.
A program may use at most 64 MiB of HBM per device.

v0:
```python
import math
import jax
import jax.numpy as jnp
from jax import lax
from jax.sharding import PartitionSpec as P

SWEEPS = 2
HIGH = lax.Precision.HIGHEST


def kernel_turned(rows, row_norms, lands):
    wide = lands.astype(jnp.float32)
    land_norms = jnp.sum(wide * wide, axis=1)
    cross = lax.dot_general(
        lands, rows, (((1,), (1,)), ((), ())), preferred_element_type=jnp.float32
    )
    dist = land_norms[:, None] + row_norms[None, :] - 2.0 * cross
    return jnp.exp(-dist * (2.0 / rows.shape[1]))


def column_fold(rows, row_norms, weighted):

    def fold(total, piece, start):
        count = piece.shape[0]
        width = math.gcd(count, 512)

        def step_block(j, acc):
            lands = lax.dynamic_slice_in_dim(piece, j * width, width, 0)
            block = kernel_turned(rows, row_norms, lands)
            part = jnp.dot(block, weighted, precision=HIGH, preferred_element_type=jnp.float32)
            return lax.dynamic_update_slice_in_dim(acc, part, j * width, 0)

        return lax.fori_loop(0, count // width, step_block, total)

    return fold


def row_fold(rows, row_norms, mixing):

    def fold(total, piece, start):
        count = piece.shape[0]
        width = math.gcd(count, 512)

        def step_block(j, acc):
            lands = lax.dynamic_slice_in_dim(piece, j * width, width, 0)
            block = kernel_turned(rows, row_norms, lands)
            mix = lax.dynamic_slice_in_dim(mixing, j * width, width, 0)
            return acc + lax.dot_general(
                block,
                mix,
                (((0,), (0,)), ((), ())),
                precision=HIGH,
                preferred_element_type=jnp.float32,
            )

        return lax.fori_loop(0, count // width, step_block, total)

    return fold


def over_columns(rows, row_norms, weighted, own_lands):
    total_lands = own_lands.shape[0] * lax.axis_size("traj")
    start = jnp.zeros((total_lands, weighted.shape[1]), jnp.float32)
    fold = column_fold(rows, row_norms, weighted)
    return fold(start, lax.all_gather(own_lands, "traj", axis=0, tiled=True), jnp.int32(0))


def over_rows(rows, row_norms, mixing, own_lands):
    start = jnp.zeros((rows.shape[0], mixing.shape[1]), jnp.float32)
    fold = row_fold(rows, row_norms, mixing)
    return fold(start, lax.all_gather(own_lands, "traj", axis=0, tiled=True), jnp.int32(0))


def orthonormal(block, gram):
    lower = jnp.linalg.cholesky(gram)
    return jax.scipy.linalg.solve_triangular(lower, block.T, lower=True).T


def orthonormal_upper(block, gram):
    return orthonormal(block[:, ::-1], gram[::-1, ::-1])[:, ::-1]


def landmark_reduce(partial_value, scale_all):
    total = lax.psum(partial_value, "traj")
    return total / scale_all


def local(trajectories, landmark_index, start_vectors):
    row_dev = trajectories.shape[0]
    wide_rows = trajectories.astype(jnp.float32)
    row_norms = jnp.sum(wide_rows * wide_rows, axis=1)
    local_index = landmark_index - lax.axis_index("traj") * row_dev
    own_lands = jnp.take(trajectories, local_index, axis=0)
    own_norms = jnp.take(row_norms, local_index, axis=0)
    total_lands = own_lands.shape[0] * lax.axis_size("traj")
    land_deg = over_rows(own_lands, own_norms, jnp.ones((total_lands, 1), jnp.float32), own_lands)
    deg_all = lax.all_gather(land_deg, "traj", axis=0, tiled=True)
    col_part = over_columns(trajectories, row_norms, jnp.ones((row_dev, 1), jnp.float32), own_lands)
    ratio = landmark_reduce(col_part, deg_all)
    degree = over_rows(trajectories, row_norms, ratio, own_lands)
    dinv = lax.rsqrt(degree)
    vectors = start_vectors
    gram_part = None
    for sweep in range(SWEEPS):
        if gram_part is not None:
            gram = lax.psum(gram_part, "traj")
            vectors = orthonormal_upper(vectors, gram)
        partial_value = over_columns(trajectories, row_norms, dinv * vectors, own_lands)
        scaled = landmark_reduce(partial_value, deg_all)
        vectors = dinv * over_rows(trajectories, row_norms, scaled, own_lands)
        gram_part = jnp.dot(vectors.T, vectors, precision=HIGH, preferred_element_type=jnp.float32)
    gram = lax.psum(gram_part, "traj")
    vectors = orthonormal(vectors, gram)
    return math.sqrt(row_dev * lax.axis_size("traj")) * vectors


def solution(mesh):
    return jax.shard_map(
        local,
        mesh=mesh,
        in_specs=(P(("groups", "traj"), None), P(("groups", "traj")), P(("groups", "traj"), None)),
        out_specs=P(("groups", "traj"), None),
        check_vma=False,
    )
```

profile of v0, /device:TPU:0, one launch (start us, length us, event | category | flops | bytes accessed | tf_op | source)
XLA Modules:
  0.0 389.3 jit_solution(15879041102556417802)
XLA Ops:
  6.5 1.1 multiply_reduce_fusion.1
  7.8 0.6 copy-done.2
  8.4 0.7 gather_fusion.1
  9.8 23.8 %all_gather.4 = bf16[512,192]{1,0:T(8,128)(2,1)S(1)} all-gather(bf16[32,192]{1,0:T(8,128)(2,1)S(1)} %broadcast_select_fusion), channel_id=1, replica_groups=mesh['groups'=2,'traj'=16] {'traj'}, dimensions={0}, use_global_device_ids=true | all-gather | bytes 208896 | tf_op jit(solution)/shard_map/all_gather | solution.py:71
  34.6 1.0 convolution_bitcast_fusion.1
  37.1 29.8 %all-reduce.1 = (f32[512,1]{0,1:T(1,128)S(1)}, f32[512]{0:T(512)S(1)}) all-reduce(f32[512,1]{0,1:T(1,128)S(1)} %convolution_bitcast_fusion.1, f32[512]{0:T(512)S(1)} %dynamic-update-slice.2), channel_id=1, replica_groups=mesh['groups'=2,'traj'=16] {'traj'}, use_global_device_ids=true, to_apply=%region_2.3 | all-reduce | flops 1024 | bytes 8192 | tf_op jit(solution)/shard_map/psum | solution.py:84
  66.9 0.7 fusion.29
  67.8 1.7 fusion.17
  69.5 86.2 %all-reduce.5.cloned.1.call-done = f32[512,32]{1,0:T(8,128)} async-done(((f32[512,32]{1,0:T(8,128)}), f32[512,32]{1,0:T(8,128)}) %all-reduce.5.cloned.1.call-update) | async-done | bytes 65552 | tf_op jit(solution)/shard_map/psum | solution.py:84
  155.7 1.7 convolution_multiply_fusion.4
  157.8 60.0 %psum.37 = f32[32,32]{0,1:T(8,128)S(1)} all-reduce(f32[32,32]{0,1:T(8,128)S(1)} %rev.9), channel_id=1, replica_groups=mesh['groups'=2,'traj'=16] {'traj'}, use_global_device_ids=true, to_apply=%region_4.5 | all-reduce | flops 1024 | bytes 8192 | tf_op jit(solution)/shard_map/psum | solution.py:106
  217.9 2.9 cholesky.44
  220.9 0.6 compare_reduce_fusion.1
  221.5 0.7 fusion.21
  222.2 2.5 custom-call.6
  225.0 1.7 fusion.15
  226.7 86.2 %all-reduce.7.cloned.1.call-done = f32[512,32]{1,0:T(8,128)} async-done(((f32[512,32]{1,0:T(8,128)}), f32[512,32]{1,0:T(8,128)}) %all-reduce.7.cloned.1.call-update) | async-done | bytes 65552 | tf_op jit(solution)/shard_map/psum | solution.py:84
  312.9 1.7 convolution_multiply_fusion.3
  314.8 60.0 %psum.39 = f32[32,32]{0,1:T(8,128)S(1)} all-reduce(f32[32,32]{0,1:T(8,128)S(1)} %fusion.36), channel_id=1, replica_groups=mesh['groups'=2,'traj'=16] {'traj'}, use_global_device_ids=true, to_apply=%region_8.11 | all-reduce | flops 1024 | bytes 8192 | tf_op jit(solution)/shard_map/psum | solution.py:112
  374.9 2.9 cholesky.55
  377.8 0.6 compare_reduce_fusion
  378.5 0.7 fusion.22
  379.1 2.4 custom-call.7
  381.6 0.9 fusion.8
  (37 shorter events, 4.1 us)
Async XLA Ops:
  6.5 1.1 copy-start
  6.5 149.2 %all-reduce.5.cloned.1.call-start = ((), (), s32[]{:S(2)}) async-start(), calls=%async_computation | async-start | bytes 524288 | tf_op jit(solution)/shard_map/psum | solution.py:84
  7.7 0.7 copy-start.2
  34.6 1.0 copy-start.3
  66.9 0.8 copy-start.1
  69.5 243.4 %all-reduce.7.cloned.1.call-start = ((), (), s32[]{:S(2)}) async-start(), calls=%async_computation.1 | async-start | bytes 524288 | tf_op jit(solution)/shard_map/psum | solution.py:84
Sparse Core Ops, SparseCore 0:
  69.6 86.0 all-reduce.4
  226.8 85.9 all-reduce.6
where the time goes:
time: 390 us; the launch traced here: 389 us
  blocking collectives  174 us (45%)
  waiting for transfers between devices  172 us (44%)
  other arithmetic  14.7 us (4%)
  between operations  14.2 us (4%)
  matrix products  10.9 us (3%)
    psum x2, waiting for transfers between devices, landmark_reduce(): total = lax.psum(partial_value, 'traj')  172 us
    psum x2, blocking collectives, local(): gram = lax.psum(gram_part, 'traj')  120 us
    psum x1, blocking collectives, landmark_reduce(): total = lax.psum(partial_value, 'traj')  29.8 us
    all_gather x1, blocking collectives, over_rows(): lax.all_gather(own_lands, 'traj', axis=0, tiled=True)  23.8 us
  transfers between devices with their start and end apart: 2, of which 2 were waited for; matrix products, arithmetic and copies ran while one was open for 0% of the time, Pallas kernels for 0%

commit v1 on v0

--- a/solution.py
+++ b/solution.py
@@ -81,7 +81,7 @@
 
 
 def landmark_reduce(partial_value, scale_all):
-    total = lax.psum(partial_value, "traj")
+    total = jnp.sum(lax.all_gather(partial_value, "traj"), axis=0)
     return total / scale_all
 
 

time: 390 us -> 308 us (0.79)
  waiting for transfers between devices: 172 us -> 72.2 us
  blocking collectives: 174 us -> 190 us
  local copies, waits for them, and re-layouts: 3.58 us -> 7.74 us
    psum x2 -> x0, waiting for transfers between devices: 172 us -> none  [landmark_reduce(): total = lax.psum(partial_value, 'traj')]
    all_gather x0 -> x2, waiting for transfers between devices: none -> 72.2 us  [landmark_reduce(): total = jnp.sum(lax.all_gather(partial_value, 'traj'), axis=0)]
    unnamed x0 -> x1, blocking collectives: none -> 29.8 us
    psum x1 -> x0, blocking collectives: 29.8 us -> none  [landmark_reduce(): total = lax.psum(partial_value, 'traj')]
    all_gather x0 -> x1, blocking collectives: none -> 17.2 us  [landmark_reduce(): total = jnp.sum(lax.all_gather(partial_value, 'traj'), axis=0)]
    unnamed x12 -> x14, local copies, waits for them, and re-layouts: 1.81 us -> 5.97 us
where the time goes in v1:
time: 308 us
  blocking collectives  190 us (62%)
  waiting for transfers between devices  72.2 us (23%)
  other arithmetic  15.1 us (5%)
  between operations  14.2 us (5%)
  matrix products  8.79 us (3%)
  local copies, waits for them, and re-layouts  7.74 us (3%)
    psum x2, blocking collectives, local(): gram = lax.psum(gram_part, 'traj')  119 us
    all_gather x2, waiting for transfers between devices, landmark_reduce(): total = jnp.sum(lax.all_gather(partial_value, 'traj'), axis=0)  72.2 us
    unnamed x1, blocking collectives  29.8 us
    all_gather x1, blocking collectives, over_rows(): lax.all_gather(own_lands, 'traj', axis=0, tiled=True)  23.8 us
    all_gather x1, blocking collectives, landmark_reduce(): total = jnp.sum(lax.all_gather(partial_value, 'traj'), axis=0)  17.2 us
    another operation x6, other arithmetic, orthonormal(): lower = jnp.linalg.cholesky(gram)  7.19 us
    another operation x4, other arithmetic, orthonormal(): return jax.scipy.linalg.solve_triangular(lower, block.T, lower=True).T  6.2 us
  transfers between devices with their start and end apart: 2, of which 2 were waited for; matrix products, arithmetic and copies ran while one was open for 0% of the time, Pallas kernels for 0%

profile of v1, /device:TPU:0, one launch (start us, length us, event | category | flops | bytes accessed | tf_op | source)
XLA Modules:
  0.0 308.1 jit_solution(3951639262392159583)
XLA Ops:
  6.5 1.1 multiply_reduce_fusion.1
  8.4 0.7 gather_fusion.1
  9.8 23.8 %all_gather.30 = bf16[512,192]{1,0:T(8,128)(2,1)S(1)} all-gather(bf16[32,192]{1,0:T(8,128)(2,1)S(1)} %broadcast_select_fusion), channel_id=1, replica_groups=mesh['groups'=2,'traj'=16] {'traj'}, dimensions={0}, use_global_device_ids=true | all-gather | bytes 208896 | tf_op jit(solution)/shard_map/all_gather | solution.py:71
  36.5 29.8 %all-reduce = f32[512]{0:T(512)S(1)} all-reduce(f32[512]{0:T(512)S(1)} %dynamic-update-slice.2), channel_id=3, replica_groups=mesh['groups'=2,'traj'=16] {'traj'}, use_global_device_ids=true, to_apply=%add | all-reduce | flops 512 | bytes 4096
  66.3 1.0 convolution_bitcast_fusion.1
  67.3 17.2 %all-gather.4 = f32[16,1,512]{2,1,0:T(1,128)S(1)} all-gather(f32[1,1,512]{2,1,0:T(1,128)S(1)} %convolution_bitcast_fusion.1), channel_id=2, replica_groups=mesh['groups'=2,'traj'=16] {'traj'}, dimensions={0}, use_global_device_ids=true | all-gather | bytes 34816 | tf_op jit(solution)/shard_map/all_gather | solution.py:84
  84.5 0.6 fusion.33
  85.4 1.7 fusion.15
  87.2 36.8 %all-gather.8.cloned.1.call-done = f32[8192,32]{0,1:T(8,128)} async-done(((f32[512,32]{0,1:T(8,128)}), f32[8192,32]{0,1:T(8,128)}) %all-gather.8.cloned.1.call-update) | async-done | bytes 1048592 | tf_op jit(solution)/shard_map/all_gather | solution.py:84
  124.0 1.8 copy.21
  126.0 0.7 convolution_multiply_fusion.3
  127.1 59.6 %psum.14 = f32[32,32]{0,1:T(8,128)S(1)} all-reduce(f32[32,32]{0,1:T(8,128)S(1)} %rev.9), channel_id=1, replica_groups=mesh['groups'=2,'traj'=16] {'traj'}, use_global_device_ids=true, to_apply=%region_4.5 | all-reduce | flops 1024 | bytes 8192 | tf_op jit(solution)/shard_map/psum | solution.py:106
  186.8 2.9 cholesky.44
  190.4 0.7 fusion.21
  191.1 2.5 custom-call.6
  193.9 1.7 fusion.12
  195.6 35.4 %all-gather.10.cloned.1.call-done = f32[8192,32]{0,1:T(8,128)} async-done(((f32[512,32]{0,1:T(8,128)}), f32[8192,32]{0,1:T(8,128)}) %all-gather.10.cloned.1.call-update) | async-done | bytes 1048592 | tf_op jit(solution)/shard_map/all_gather | solution.py:84
  231.0 1.8 copy.22
  233.0 0.7 convolution_multiply_fusion.2
  233.9 59.6 %psum.15 = f32[32,32]{0,1:T(8,128)S(1)} all-reduce(f32[32,32]{0,1:T(8,128)S(1)} %fusion.35), channel_id=1, replica_groups=mesh['groups'=2,'traj'=16] {'traj'}, use_global_device_ids=true, to_apply=%region_8.11 | all-reduce | flops 1024 | bytes 8192 | tf_op jit(solution)/shard_map/psum | solution.py:112
  293.6 2.9 cholesky.55
  297.2 0.7 fusion.22
  297.9 2.4 custom-call.7
  300.3 0.9 fusion.4
  (44 shorter events, 6.7 us)
Async XLA Ops:
  6.5 1.1 copy-start
  6.5 117.4 %all-gather.8.cloned.1.call-start = ((), (), s32[]{:S(2)}) async-start(), calls=%async_computation | async-start | bytes 1114112 | tf_op jit(solution)/shard_map/all_gather | solution.py:84
  7.7 0.7 copy-start.2
  34.3 0.7 copy-start.3
  84.5 0.8 copy-start.1
  87.1 143.9 %all-gather.10.cloned.1.call-start = ((), (), s32[]{:S(2)}) async-start(), calls=%async_computation.1 | async-start | bytes 1114112 | tf_op jit(solution)/shard_map/all_gather | solution.py:84
Sparse Core Ops, SparseCore 0:
  87.2 36.6 all-gather.7
  195.7 35.2 all-gather.9
